TPU v7x, 256 devices: a whole 4x4x8 slice. The times are simulated.
256 devices in a mesh: pipe: 8 (over y, x_lo), expert: 32 (over z, x_hi, core).
Axes of the slice: x: 4 (x_hi: 2, x_lo: 2; x = x_hi * 2 + x_lo), y: 4, z: 8, core: 2. Of those that a mesh axis runs over, the one named last changes fastest.
Arguments:
- fwd_prev: bfloat16 [8, 4096, 3584], P('pipe', 'expert'), may hold values from -6 to 6
- bwd_next: bfloat16 [8, 4096, 3584], P('pipe', 'expert'), may hold values from -6 to 6
- bwd_input: bfloat16 [8, 4096, 3584], P('pipe', 'expert'), may hold values from -6 to 6
- norm_gain: float32 [8, 3584], P('pipe'), may hold values from 0.1 to 1.9
- w_gate: bfloat16 [8, 3584, 8192], P('pipe', None, 'expert'), may hold values from -0.09375 to 0.09375
- w_up: bfloat16 [8, 3584, 8192], P('pipe', None, 'expert'), may hold values from -0.09375 to 0.09375
- w_down: bfloat16 [8, 8192, 3584], P('pipe', 'expert'), may hold values from -0.375 to 0.375
- fwd_routes: int32 [8, 4096, 1], P('pipe', 'expert'), may hold values from 0 to 7; in each aligned block of 128 rows (0 to 127, 128 to 255, ..., all dimensions but the last counted through in order) at most 24 rows name the same one
- fwd_gates: float32 [8, 4096, 1], P('pipe', 'expert'), may hold values from 0.2 to 1
- bwd_routes: int32 [8, 4096, 1], P('pipe', 'expert'), may hold values from 0 to 7; in each aligned block of 128 rows (0 to 127, 128 to 255, ..., all dimensions but the last counted through in order) at most 24 rows name the same one
- bwd_gates: float32 [8, 4096, 1], P('pipe', 'expert'), may hold values from 0.2 to 1
Outputs:
- fwd_out: bfloat16 [8, 4096, 3584], P('pipe', 'expert')
- bwd_grad: bfloat16 [8, 4096, 3584], P('pipe', 'expert')
- gain_grad: float32 [8, 3584], P('pipe')
Inputs may be any that keep to these rules, and one draw needn't show every extreme that they name: `fwd_routes`: within each device's 128 tokens (one aligned block of rows), a token's 1 picks are different experts and no expert is picked more than 24 times. `bwd_routes`: within each device's 128 tokens (one aligned block of rows), a token's 1 picks are different experts and no expert is picked more than 24 times.
All inputs are finite; a program needn't handle non-finite values.
Results may differ from a plain program's by a relative error of at most 0.0067.
Values may be sent and summed in bfloat16 or wider, within the bound.
A program may use at most 128 MiB of HBM per device.

v0:
```python
import jax
import jax.numpy as jnp
from jax import lax
from jax.sharding import PartitionSpec as P

EXPERTS = 8
TOP = 1
CAP = 24


EPS = 1e-06


def from_behind(block, axis, distance):
    devices = range(lax.axis_size(axis))
    route = [((i - distance) % len(devices), i) for i in devices]
    return lax.ppermute(block, axis, route)


def normalize(hidden_in, gain_vec):
    values = hidden_in.astype(jnp.float32)
    inverse = lax.rsqrt(jnp.mean(values * values, axis=-1, keepdims=True) + EPS)
    normed = (values * inverse * gain_vec).astype(jnp.bfloat16)
    return (values, inverse, normed)


def slot_index(route_block):
    experts_of = route_block.reshape(-1)
    onehot = (experts_of[:, None] == jnp.arange(EXPERTS, dtype=jnp.int32)[None, :]).astype(
        jnp.int32
    )
    before = jnp.cumsum(onehot, axis=0) - onehot
    position = jnp.sum(before * onehot, axis=1)
    return experts_of * CAP + position


def dispatch_rows(slot_ids, row_data):
    selector = (jnp.arange(EXPERTS * CAP, dtype=jnp.int32)[:, None] == slot_ids[None, :]).astype(
        row_data.dtype
    )
    return jnp.dot(selector, row_data, preferred_element_type=jnp.float32).astype(jnp.bfloat16)


def spread_out(buffer_rows, split_count):
    columns = buffer_rows.shape[-1]
    grouped = buffer_rows.reshape(EXPERTS, 1, CAP, columns)
    return jnp.broadcast_to(grouped, (EXPERTS, split_count, CAP, columns)).reshape(
        EXPERTS * split_count, CAP, columns
    )


def contract_last(left, right):
    return lax.dot_general(
        left, right, (((1,), (1,)), ((), ())), preferred_element_type=jnp.float32
    )


def expert_forward(row_data, gate_w, up_w, down_w):
    gate_pre = jnp.dot(row_data, gate_w, preferred_element_type=jnp.float32)
    up_pre = jnp.dot(row_data, up_w, preferred_element_type=jnp.float32)
    hidden = (jax.nn.silu(gate_pre) * up_pre).astype(jnp.bfloat16)
    return jnp.dot(hidden, down_w, preferred_element_type=jnp.float32).astype(jnp.bfloat16)


def silu_grads(row_data, grad_rows, gate_w, up_w, down_w):
    gate_pre = jnp.dot(row_data, gate_w, preferred_element_type=jnp.float32)
    up_pre = jnp.dot(row_data, up_w, preferred_element_type=jnp.float32)
    hidden_grad = contract_last(grad_rows, down_w)
    sig_val = jax.nn.sigmoid(gate_pre)
    gate_grad = (hidden_grad * up_pre * sig_val * (1.0 + gate_pre * (1.0 - sig_val))).astype(
        jnp.bfloat16
    )
    up_grad = (hidden_grad * gate_pre * sig_val).astype(jnp.bfloat16)
    return (gate_grad, up_grad)


def expert_backward(row_data, grad_rows, gate_w, up_w, down_w):
    gate_grad, up_grad = silu_grads(row_data, grad_rows, gate_w, up_w, down_w)
    input_part = contract_last(gate_grad, gate_w) + contract_last(up_grad, up_w)
    return input_part.astype(jnp.bfloat16)


def collect(returned, slot_ids):
    columns = returned.shape[-1]
    summed = jnp.sum(returned.reshape(EXPERTS, -1, CAP, columns).astype(jnp.float32), axis=1)
    return jnp.take(summed.reshape(EXPERTS * CAP, columns), slot_ids, axis=0).reshape(
        -1, TOP, columns
    )


def norm_backward(values, inverse, gain_vec, normed_grad, grad_out):
    scaled_grad = normed_grad * gain_vec
    inner_sum = jnp.mean(scaled_grad * values, axis=-1, keepdims=True)
    input_grad = (
        grad_out.astype(jnp.float32)
        + inverse * scaled_grad
        - values * inverse * inverse * inverse * inner_sum
    )
    return (input_grad.astype(jnp.bfloat16), jnp.sum(normed_grad * values * inverse, axis=0))


def body(
    fwd_prev,
    bwd_next,
    bwd_input,
    norm_gain,
    w_gate,
    w_up,
    w_down,
    fwd_routes,
    fwd_gates,
    bwd_routes,
    bwd_gates,
):
    split_count = lax.axis_size("expert") // EXPERTS
    gain_vec = norm_gain[0]
    gate_w = w_gate[0]
    up_w = w_up[0]
    down_w = w_down[0]
    fwd_in = from_behind(fwd_prev[0], "pipe", 1)
    grad_in = from_behind(bwd_next[0], "pipe", -1)
    f_values, f_inverse, f_normed = normalize(fwd_in, gain_vec)
    f_slots = slot_index(fwd_routes[0])
    f_rows = dispatch_rows(f_slots, jnp.repeat(f_normed, TOP, axis=0))
    b_values, b_inverse, b_normed = normalize(bwd_input[0], gain_vec)
    b_slots = slot_index(bwd_routes[0])
    b_scaled = (grad_in.astype(jnp.float32)[:, None, :] * bwd_gates[0][:, :, None]).astype(
        jnp.bfloat16
    )
    b_scaled = b_scaled.reshape(-1, b_scaled.shape[-1])
    b_norm_rows = dispatch_rows(b_slots, jnp.repeat(b_normed, TOP, axis=0))
    b_grad_rows = dispatch_rows(b_slots, b_scaled)
    received = lax.all_to_all(
        spread_out(f_rows, split_count), "expert", split_axis=0, concat_axis=0, tiled=True
    )
    columns = received.shape[-1]
    result = expert_forward(received.reshape(-1, columns), gate_w, up_w, down_w)
    f_partial = result.reshape(received.shape)
    f_back = lax.all_to_all(f_partial, "expert", split_axis=0, concat_axis=0, tiled=True)
    received = (
        lax.all_to_all(
            spread_out(b_norm_rows, split_count), "expert", split_axis=0, concat_axis=0, tiled=True
        ),
        lax.all_to_all(
            spread_out(b_grad_rows, split_count), "expert", split_axis=0, concat_axis=0, tiled=True
        ),
    )
    received_norm = received[0]
    columns = received_norm.shape[-1]
    result = expert_backward(
        received_norm.reshape(-1, columns), received[1].reshape(-1, columns), gate_w, up_w, down_w
    )
    b_partial = result.reshape(received_norm.shape)
    b_back = lax.all_to_all(b_partial, "expert", split_axis=0, concat_axis=0, tiled=True)
    f_picked = collect(f_back, f_slots)
    b_picked = collect(b_back, b_slots)
    moe_out = jnp.sum(f_picked * fwd_gates[0][:, :, None], axis=1)
    fwd_out = (f_values + moe_out).astype(jnp.bfloat16)
    normed_grad = jnp.sum(b_picked, axis=1)
    bwd_grad, gain_part = norm_backward(b_values, b_inverse, gain_vec, normed_grad, grad_in)
    gain_grad = lax.psum(gain_part, "expert")
    return (fwd_out[None], bwd_grad[None], gain_grad[None])


def solution(mesh):
    placed = (
        P("pipe", "expert", None),
        P("pipe", "expert", None),
        P("pipe", "expert", None),
        P("pipe", None),
        P("pipe", None, "expert"),
        P("pipe", None, "expert"),
        P("pipe", "expert", None),
        P("pipe", "expert", None),
        P("pipe", "expert", None),
        P("pipe", "expert", None),
        P("pipe", "expert", None),
    )
    return jax.shard_map(
        body,
        mesh=mesh,
        in_specs=placed,
        out_specs=(P("pipe", "expert", None), P("pipe", "expert", None), P("pipe", None)),
        check_vma=False,
    )
```

profile of v0, /device:TPU:10, one launch (start us, length us, event | category | flops | bytes accessed | tf_op | source)
XLA Modules:
  0.0 800.2 jit_solution(4018591856126203406)
XLA Ops:
  0.6 0.0 copy-start
  0.6 0.9 fusion.74
  1.5 0.2 reduce_window_sum.18
  1.7 0.8 select_reduce_fusion
  2.5 0.7 compare_and_fusion
  3.2 1.4 fusion.12
  4.7 0.8 reduce
  5.4 1.8 convolution_convert_fusion.1
  7.2 2.8 broadcast_in_dim.57
  10.0 0.0 copy-start.10
  10.0 0.0 copy-start.8
  10.0 10.7 %all-to-all-start.3 = ((bf16[32,24,3584]{2,1,0:T(8,128)(2,1)}), bf16[32,24,3584]{2,1,0:T(8,128)(2,1)}, u32[]{:S(2)}, u32[]{:S(2)}) async-start(bf16[32,24,3584]{2,1,0:T(8,128)(2,1)} %bitcast.90), calls=%async_computation.3 | async-start | bytes 11010048 | tf_op jit(solution)/shard_map/all_to_all | solution.py:141
  20.7 0.0 copy-done.10
  20.7 1.5 collective-permute-start.1
  22.2 55.0 %collective-permute-done.1 = bf16[128,3584]{1,0:T(8,128)(2,1)S(1)} collective-permute-done((bf16[128,3584]{1,0:T(8,128)(2,1)S(1)}, bf16[128,3584]{1,0:T(8,128)(2,1)S(1)}, u32[]{:S(2)}, u32[]{:S(2)}) %collective-permute-start.1) | collective-permute-done | bytes 917536 | tf_op jit(solution)/shard_map/ppermute | solution.py:17
  77.2 0.0 copy-start.5
  77.2 0.9 copy-done.5
  78.1 0.0 copy-done.8
  78.1 0.6 convolution_convert_fusion.2
  78.7 66.8 %all-to-all-done.3 = bf16[32,24,3584]{2,1,0:T(8,128)(2,1)} async-done(((bf16[32,24,3584]{2,1,0:T(8,128)(2,1)}), bf16[32,24,3584]{2,1,0:T(8,128)(2,1)}, u32[]{:S(2)}, u32[]{:S(2)}) %all-to-all-start.3) | async-done | bytes 5505056 | tf_op jit(solution)/shard_map/all_to_all | solution.py:141
  145.6 2.9 broadcast_in_dim.55
  148.4 0.0 copy-start.6
  148.4 5.0 all-to-all-start.2
  153.4 2.5 collective-permute-start
  156.0 0.0 copy-done.6
  156.0 0.1 fusion.75
  156.1 0.2 reduce_window_sum.17
  156.2 0.2 select_reduce_fusion.1
  156.4 52.5 %collective-permute-done = bf16[128,3584]{1,0:T(8,128)(2,1)S(1)} collective-permute-done((bf16[128,3584]{1,0:T(8,128)(2,1)}, bf16[128,3584]{1,0:T(8,128)(2,1)S(1)}, u32[]{:S(2)}, u32[]{:S(2)}) %collective-permute-start) | collective-permute-done | bytes 917536 | tf_op jit(solution)/shard_map/ppermute | solution.py:17
  208.9 0.0 copy-start.2
  208.9 0.3 fusion.8
  209.2 1.7 convolution_convert_fusion.3
  210.9 67.4 %all-to-all-done.2 = bf16[32,24,3584]{2,1,0:T(8,128)(2,1)} async-done(((bf16[32,24,3584]{2,1,0:T(8,128)(2,1)}), bf16[32,24,3584]{2,1,0:T(8,128)(2,1)}, u32[]{:S(2)}, u32[]{:S(2)}) %all-to-all-start.2) | async-done | bytes 5505056 | tf_op jit(solution)/shard_map/all_to_all | solution.py:144
  278.3 4.2 broadcast_in_dim.28
  282.5 0.0 copy-done.2
  282.5 5.1 all-to-all-start
  287.5 0.0 copy-start.9
  287.5 4.8 fusion.26
  292.4 0.0 copy-done.9
  292.4 4.2 fusion.16
  296.6 0.0 copy-done
  296.6 13.1 %fusion.24 = f32[768,3584]{1,0:T(8,128)} fusion(bf16[1,3584,256]{2,1,0:T(8,128)(2,1)} %param.17, f32[768,256]{1,0:T(8,128)S(1)} %fusion.16, bf16[768,3584]{1,0:T(8,128)(2,1)} %bitcast.23, bf16[1,3584,256]{2,1,0:T(8,128)(2,1)S(1)} %copy-done, f32[768,256]{1,0:T(8,128)S(1)} %fusion.26), kind=kOutput, calls=%fused_computation.42 | convolution fusion | flops 2820538368 | bytes 21757952 | tf_op jit(solution)/shard_map/dot_general | solution.py:53
  309.7 8.2 %add_convert_fusion = bf16[768,3584]{1,0:T(8,128)(2,1)} fusion(f32[768,3584]{1,0:T(8,128)} %fusion.24, bf16[1,3584,256]{2,1,0:T(8,128)(2,1)S(1)} %copy-done, f32[768,256]{1,0:T(8,128)S(1)} %fusion.16, f32[768,256]{1,0:T(8,128)S(1)} %fusion.26), kind=kOutput, calls=%fused_computation.4 | convolution fusion | flops 1415970816 | bytes 19922944 | tf_op jit(solution)/shard_map/dot_general | solution.py:53
  317.8 94.3 %all-to-all-done = bf16[32,24,3584]{2,1,0:T(8,128)(2,1)} async-done(((bf16[32,24,3584]{2,1,0:T(8,128)(2,1)}), bf16[32,24,3584]{2,1,0:T(8,128)(2,1)}, u32[]{:S(2)}, u32[]{:S(2)}) %all-to-all-start) | async-done | bytes 5505056 | tf_op jit(solution)/shard_map/all_to_all | solution.py:133
  412.2 5.1 all-to-all-start.4
  417.3 4.7 fusion.28
  422.0 11.3 %convolution_convert_fusion = bf16[768,3584]{1,0:T(8,128)(2,1)} fusion(bf16[1,256,3584]{2,1,0:T(8,128)(2,1)} %param.19, bf16[768,3584]{1,0:T(8,128)(2,1)} %bitcast.4, bf16[1,3584,256]{2,1,0:T(8,128)(2,1)S(1)} %copy-done, f32[768,256]{1,0:T(8,128)S(1)} %fusion.28), kind=kOutput, calls=%fused_computation.5 | convolution fusion | flops 2822504448 | bytes 15466496 | tf_op jit(solution)/shard_map/dot_general | solution.py:62
  433.3 108.6 %all-to-all-done.4 = bf16[32,24,3584]{2,1,0:T(8,128)(2,1)} async-done(((bf16[32,24,3584]{2,1,0:T(8,128)(2,1)}), bf16[32,24,3584]{2,1,0:T(8,128)(2,1)}, u32[]{:S(2)}, u32[]{:S(2)}) %all-to-all-start.4) | async-done | bytes 5505056 | tf_op jit(solution)/shard_map/all_to_all | solution.py:154
  541.9 4.9 all-to-all-start.1
  546.9 5.2 convert_reduce_fusion
  552.1 0.0 copy-start.1
  552.1 5.0 gather_fusion.1
  557.1 0.0 copy-done.1
  557.1 2.2 fusion.15
  559.3 225.8 %psum.7 = f32[1,3584]{1,0:T(1,128)} all-reduce(f32[1,3584]{1,0:T(1,128)S(1)} %broadcast_in_dim.59), channel_id=1, replica_groups=mesh['pipe'=8,'expert'=32] {'expert'}, use_global_device_ids=true, to_apply=%region_10.12 | all-reduce | flops 3584 | bytes 28672 | tf_op jit(solution)/shard_map/psum | solution.py:161
  785.1 0.0 all-to-all-done.1
  785.1 5.2 convert_reduce_fusion.1
  790.3 4.9 gather_fusion
  795.2 0.0 copy-start.3
  795.3 3.7 fusion.62
  798.9 0.0 copy-done.3
  798.9 0.0 copy-done.4
  798.9 0.0 copy-done.7
  798.9 1.3 fusion.52
  (11 shorter events, 0.1 us)
Async XLA Ops:
  0.6 295.9 %copy-start = (bf16[1,3584,256]{2,1,0:T(8,128)(2,1)S(1)}, bf16[1,3584,256]{2,1,0:T(8,128)(2,1)}, u32[]{:S(2)}) copy-start(bf16[1,3584,256]{2,1,0:T(8,128)(2,1)} %param.18) | copy-start | bytes 5505028
  10.0 10.7 %copy-start.10 = (bf16[1,128,3584]{2,1,0:T(8,128)(2,1)S(1)}, bf16[1,128,3584]{2,1,0:T(8,128)(2,1)}, u32[]{:S(2)}) copy-start(bf16[1,128,3584]{2,1,0:T(8,128)(2,1)} %param.14) | copy-start | bytes 2752516
  10.0 68.1 %copy-start.8 = (f32[1,128,1]{1,2,0:T(1,128)S(1)}, f32[1,128,1]{1,2,0:T(1,128)}, u32[]{:S(2)}) copy-start(f32[1,128,1]{1,2,0:T(1,128)} %param.23) | copy-start | bytes 1540
  10.0 135.6 %all-to-all-start.3 = ((bf16[32,24,3584]{2,1,0:T(8,128)(2,1)}), bf16[32,24,3584]{2,1,0:T(8,128)(2,1)}, u32[]{:S(2)}, u32[]{:S(2)}) async-start(bf16[32,24,3584]{2,1,0:T(8,128)(2,1)} %bitcast.90), calls=%async_computation.3 | async-start | bytes 11010048 | tf_op jit(solution)/shard_map/all_to_all | solution.py:141
  20.7 56.5 %collective-permute-start.1 = (bf16[128,3584]{1,0:T(8,128)(2,1)S(1)}, bf16[128,3584]{1,0:T(8,128)(2,1)S(1)}, u32[]{:S(2)}, u32[]{:S(2)}) collective-permute-start(bf16[128,3584]{1,0:T(8,128)(2,1)S(1)} %bitcast.101), channel_id=1, source_target_pairs={{32,0},{64,32},{96,64},{128,96},{160,128},{192,160},{224,192},{0,2... | collective-permute-start | bytes 2752520 | tf_op jit(solution)/shard_map/ppermute | solution.py:17
  77.2 0.9 copy-start.5
  148.4 7.5 copy-start.6
  148.4 129.9 %all-to-all-start.2 = ((bf16[32,24,3584]{2,1,0:T(8,128)(2,1)}), bf16[32,24,3584]{2,1,0:T(8,128)(2,1)}, u32[]{:S(2)}, u32[]{:S(2)}) async-start(bf16[32,24,3584]{2,1,0:T(8,128)(2,1)} %bitcast.87), calls=%async_computation.2 | async-start | bytes 11010048 | tf_op jit(solution)/shard_map/all_to_all | solution.py:144
  153.4 55.5 %collective-permute-start = (bf16[128,3584]{1,0:T(8,128)(2,1)}, bf16[128,3584]{1,0:T(8,128)(2,1)S(1)}, u32[]{:S(2)}, u32[]{:S(2)}) collective-permute-start(bf16[128,3584]{1,0:T(8,128)(2,1)} %bitcast.102), channel_id=1, source_target_pairs={{224,0},{0,32},{32,64},{64,96},{96,128},{128,160},{160,192},{192,2... | collective-permute-start | bytes 2752520 | tf_op jit(solution)/shard_map/ppermute | solution.py:17
  208.9 73.5 %copy-start.2 = (bf16[128,3584]{1,0:T(8,128)(2,1)}, bf16[128,3584]{1,0:T(8,128)(2,1)S(1)}, u32[]{:S(2)}) copy-start(bf16[128,3584]{1,0:T(8,128)(2,1)S(1)} %collective-permute-done) | copy-start | bytes 2752516
  282.5 129.7 %all-to-all-start = ((bf16[32,24,3584]{2,1,0:T(8,128)(2,1)}), bf16[32,24,3584]{2,1,0:T(8,128)(2,1)}, u32[]{:S(2)}, u32[]{:S(2)}) async-start(bf16[32,24,3584]{2,1,0:T(8,128)(2,1)} %bitcast.89), calls=%async_computation | async-start | bytes 11010048 | tf_op jit(solution)/shard_map/all_to_all | solution.py:133
  287.5 4.9 copy-start.9
  412.2 129.7 %all-to-all-start.4 = ((bf16[32,24,3584]{2,1,0:T(8,128)(2,1)}), bf16[32,24,3584]{2,1,0:T(8,128)(2,1)}, u32[]{:S(2)}, u32[]{:S(2)}) async-start(bf16[32,24,3584]{2,1,0:T(8,128)(2,1)} %bitcast.88), calls=%async_computation.4 | async-start | bytes 11010048 | tf_op jit(solution)/shard_map/all_to_all | solution.py:154
  541.9 243.2 %all-to-all-start.1 = ((bf16[32,24,3584]{2,1,0:T(8,128)(2,1)}), bf16[32,24,3584]{2,1,0:T(8,128)(2,1)}, u32[]{:S(2)}, u32[]{:S(2)}) async-start(bf16[32,24,3584]{2,1,0:T(8,128)(2,1)} %bitcast.91), calls=%async_computation.1 | async-start | bytes 11010048 | tf_op jit(solution)/shard_map/all_to_all | solution.py:139
  552.1 5.1 copy-start.1
  795.2 3.7 copy-start.3
  795.3 3.7 copy-start.4
  795.3 3.7 copy-start.7
where the time goes:
time: 807 us; the launch traced here: 800 us
  waiting for transfers between devices  445 us (55%)
  blocking collectives  226 us (28%)
  matrix products  50.3 us (6%)
  starting transfers between devices  34.8 us (4%)
  other arithmetic  23 us (3%)
  local copies, waits for them, and re-layouts  20.8 us (3%)
    psum x1, blocking collectives, body(): gain_grad = lax.psum(gain_part, 'expert')  226 us
    all_to_all x1, waiting for transfers between devices, body(): lax.all_to_all(b_partial, 'expert', split_axis=0, concat_axis=0, tiled=True)  109 us
    ppermute x2, waiting for transfers between devices, from_behind(): return lax.ppermute(block, axis, route)  108 us
    all_to_all x1, waiting for transfers between devices, body(): lax.all_to_all(spread_out(f_rows, split_count), 'expert', split_axis=0, c...  94.3 us
    all_to_all x1, waiting for transfers between devices, body(): lax.all_to_all(spread_out(b_grad_rows, split_count), 'expert', split_axis...  67.4 us
    all_to_all x1, waiting for transfers between devices, body(): lax.all_to_all(spread_out(b_norm_rows, split_count), 'expert', split_axis...  66.8 us
    dot_general x3, matrix products, contract_last(): lax.dot_general(left, right, (((1,), (1,)), ((), ())), preferred_element_...  25.4 us
  transfers between devices with their start and end apart: 7, of which 6 were waited for; matrix products, arithmetic and copies ran while one was open for 8% of the time, Pallas kernels for 0%

commit v1 on v0

v1 whole, which is shorter than its diff:
```python
import jax
import jax.numpy as jnp
from jax import lax
from jax.experimental import pallas as pl
from jax.experimental.pallas import tpu as pltpu
from jax.sharding import PartitionSpec as P

MESH = pl.DeviceIdType.MESH
F32 = jnp.float32
BF16 = jnp.bfloat16

EPS = 1e-06
D = 3584
HALF = D // 2
TOK = 128
CAP = 24
ROWS = 2 * CAP
SLICE = 256
SLOTS = 8
GROUPS = SLOTS // 2
PIPE = 8

XB, DY, XF = 0, 1, 2
BWD, FWD = 0, 1

S_META = 0
S_WEIGHT = 9
S_RING = 12
S_PAIR = 36
S_DUP = 40
S_PART = 56
S_BACK = 64
S_GAIN = 80
N_SEM = 90


def dot(left, right):
    return jnp.dot(left, right, preferred_element_type=F32)


def contract_last(left, right):
    return lax.dot_general(left, right, (((1,), (1,)), ((), ())), preferred_element_type=F32)


def iota(shape, dim):
    return lax.broadcasted_iota(jnp.int32, shape, dim).astype(F32)


def halves(chunk):
    values = chunk.astype(F32)
    return values[:CAP], values[CAP:]


def inverse_rms(left, right):
    total = jnp.sum(left * left, axis=-1, keepdims=True)
    total = total + jnp.sum(right * right, axis=-1, keepdims=True)
    return lax.rsqrt(total * (1.0 / D) + EPS)


def earlier():
    return (iota((TOK, TOK), 0) < iota((TOK, TOK), 1)).astype(BF16)


def places(routes, z):
    onehot = (iota((8, TOK), 0) == routes).astype(F32)
    before = dot(onehot.astype(BF16), earlier())
    position = jnp.sum(onehot * before, axis=0, keepdims=True)
    ahead = routes - z.astype(F32)
    ahead = jnp.where(ahead < 0, ahead + 8, ahead)
    slot = jnp.where(ahead <= 4, 2 * ahead - 1, 2 * (8 - ahead))
    slot = jnp.where(ahead == 0, 0.0, slot)
    return slot * ROWS + position


def kernel(
    meta,
    gain,
    x_hbm,
    dy_hbm,
    xb_hbm,
    wg_hbm,
    wu_hbm,
    wd_hbm,
    of_hbm,
    ob_hbm,
    og_ref,
    raw,
    sent,
    landed,
    pair_xb,
    all_dy,
    all_x,
    part_out,
    part_in,
    own_part,
    final,
    back,
    outs,
    wg,
    wu,
    wd,
    normed,
    grads,
    acc,
    ring_meta,
    near_meta,
    gain_acc,
    gain_ring,
    gain_sum,
    gain_near,
    send_sem,
    recv_sem,
    local_sem,
):
    pipe = lax.axis_index("pipe")
    place = lax.axis_index("expert")
    z = place // 4
    xh = (place // 2) % 2
    core = place % 2

    def at_ring(offset):
        return {"pipe": pipe, "expert": lax.rem(z + offset + 8, 8) * 4 + xh * 2 + core}

    pair = {"pipe": pipe, "expert": z * 4 + (1 - xh) * 2 + core}
    twin = {"pipe": pipe, "expert": z * 4 + xh * 2 + (1 - core)}

    def at_section(distance, other):
        side = (1 - xh) if other else xh
        return {"pipe": lax.rem(pipe + distance + PIPE, PIPE), "expert": z * 4 + side * 2 + core}

    def remote(src, dst, sem, device):
        return pltpu.make_async_remote_copy(
            src_ref=src,
            dst_ref=dst,
            send_sem=send_sem.at[sem],
            recv_sem=recv_sem.at[sem],
            device_id=device,
            device_id_type=MESH,
        )

    loads = []
    for array, hbm in ((XB, xb_hbm), (DY, dy_hbm), (XF, x_hbm)):
        for half in range(2):
            loads.append(
                pltpu.make_async_copy(
                    hbm.at[0, :, pl.ds(half * HALF, HALF)],
                    raw.at[array, pl.ds(half * TOK, TOK)],
                    local_sem.at[array * 2 + half],
                )
            )
    for index, (hbm, vmem) in enumerate(((wg_hbm, wg), (wu_hbm, wu), (wd_hbm, wd))):
        loads.append(pltpu.make_async_copy(hbm.at[0], vmem.at[0], local_sem.at[6 + index]))
    for load in loads:
        load.start()

    barrier = pltpu.get_barrier_semaphore()
    partners = [at_ring(k) for k in range(1, 8)] + [pair, twin]
    for distance in (-1, 1):
        partners += [at_section(distance, False), at_section(distance, True)]
    for device in partners:
        pl.semaphore_signal(barrier, inc=1, device_id=device, device_id_type=MESH)
    pl.semaphore_wait(barrier, len(partners))

    def offset_of(slot):
        return (slot + 1) // 2 if slot % 2 else -(slot // 2)

    metas = [
        remote(meta, near_meta.at[0], S_META, at_section(-1, False)),
        remote(meta, near_meta.at[1], S_META + 1, at_section(1, False)),
    ]
    for slot in range(1, SLOTS):
        metas.append(
            remote(meta, ring_meta.at[slot], S_META + 1 + slot, at_ring(offset_of(slot)))
        )
    for copy in metas:
        copy.start()
    ring_meta[0] = meta[...]

    weights = [
        remote(hbm.at[0], vmem.at[1], S_WEIGHT + index, twin)
        for index, (hbm, vmem) in enumerate(((wg_hbm, wg), (wu_hbm, wu), (wd_hbm, wd)))
    ]

    def ring_copy(array, slot, offset):
        return remote(
            sent.at[array, slot],
            landed.at[array, slot],
            S_RING + array * 8 + slot,
            at_ring(offset),
        )

    def dispatch(array, routes):
        base = places(routes, z)

        def step(group, carry):
            row = iota((2 * ROWS, TOK), 0) + (group * (2 * ROWS)).astype(F32)
            picks = jnp.concatenate([row == base, row == base + CAP], axis=1)
            picks = picks.astype(F32).astype(BF16)
            rows = dot(picks, raw[array]).astype(BF16)
            sent[array, pl.ds(2 * group, 2)] = rows.reshape(2, ROWS, HALF)
            ring_copy(array, 2 * group + 1, group + 1).start()

            @pl.when(group > 0)
            def _():
                ring_copy(array, 2 * group, -group).start()

            return carry

        lax.fori_loop(0, GROUPS, step, 0)
        landed[array, 0] = sent[array, 0]

    def wait_landed(array, group):
        ring_copy(array, 2 * group + 1, group + 1).wait_recv()

        @pl.when(group > 0)
        def _():
            ring_copy(array, 2 * group, -group).wait_recv()

    loads[0].wait()
    loads[1].wait()
    dispatch(XB, meta[2:3, :])
    for copy in weights:
        copy.start()
    metas[1].wait_recv()
    loads[2].wait()
    loads[3].wait()
    dispatch(DY, near_meta[1, 2:3, :])
    metas[0].wait_recv()
    loads[4].wait()
    loads[5].wait()
    dispatch(XF, near_meta[0, 0:1, :])

    def pair_copy(group):
        two = pl.ds(2 * group, 2)
        return remote(landed.at[XB, two], pair_xb.at[two], S_PAIR + group, pair)

    def dup_copy(array, group, other):
        two = pl.ds(2 * group, 2)
        dst = all_dy if array == DY else all_x
        sem = S_DUP + (array - 1) * 8 + other * 4 + group
        device = at_section(-1 if array == DY else 1, other)
        return remote(landed.at[array, two], dst.at[other, two], sem, device)

    def relay_pair(group, carry):
        wait_landed(XB, group)
        pair_copy(group).start()
        return carry

    def relay_dup(array, group):
        wait_landed(array, group)
        dup_copy(array, group, 0).start()
        dup_copy(array, group, 1).start()

    def relay_dy(group, carry):
        relay_dup(DY, group)
        return carry

    lax.fori_loop(0, GROUPS, relay_pair, 0)
    lax.fori_loop(0, GROUPS, relay_dy, 0)

    gain_left = gain[:, :HALF]
    gain_right = gain[:, HALF:]

    def gather_rows(own, other, group, to, scaled):
        for side, ref in enumerate((own, other)):
            lefts, rights = [], []
            for s in range(2):
                left, right = halves(ref(2 * group + s))
                if scaled:
                    inverse = inverse_rms(left, right)
                    left = left * inverse * gain_left
                    right = right * inverse * gain_right
                lefts.append(left)
                rights.append(right)
            rows = pl.ds(side * ROWS, ROWS)
            to[rows, pl.ds(0, HALF)] = jnp.concatenate(lefts, axis=0).astype(BF16)
            to[rows, pl.ds(HALF, HALF)] = jnp.concatenate(rights, axis=0).astype(BF16)

    def part_copy(which, group):
        two = pl.ds(2 * group, 2)
        return remote(
            part_out.at[which, two], part_in.at[which, two], S_PART + which * 4 + group, pair
        )

    def share(which, group):
        own_part[which, group] = acc[pl.ds(0, ROWS), :]
        for s in range(2):
            rows = pl.ds(ROWS + s * CAP, CAP)
            chunk = jnp.concatenate([acc[rows, pl.ds(0, HALF)], acc[rows, pl.ds(HALF, HALF)]], axis=0)
            part_out[which, 2 * group + s] = chunk.astype(BF16)
        part_copy(which, group).start()

    for load in loads[6:]:
        load.wait()
    for copy in weights:
        copy.wait_recv()

    def backward(group, carry):
        relay_dup(XF, group)
        pair_copy(group).wait_recv()
        dup_copy(DY, group, 0).wait_recv()
        dup_copy(DY, group, 1).wait_recv()
        gather_rows(
            lambda j: landed[XB, j], lambda j: pair_xb[j], group, normed, True
        )
        gather_rows(lambda j: all_dy[0, j], lambda j: all_dy[1, j], group, grads, False)
        acc[...] = jnp.zeros_like(acc)

        def hidden(h, inner):
            rows = normed[...]
            a = dot(rows, wg[h])
            b = dot(rows, wu[h])
            dh = contract_last(grads[...], wd[h])
            sig = 1.0 / (1.0 + jnp.exp(-a))
            da = (dh * b * sig * (1.0 + a * (1.0 - sig))).astype(BF16)
            db = (dh * a * sig).astype(BF16)
            acc[...] += contract_last(da, wg[h]) + contract_last(db, wu[h])
            return inner

        lax.fori_loop(0, 2, hidden, 0)
        share(BWD, group)
        return carry

    lax.fori_loop(0, GROUPS, backward, 0)

    def gates_of(which, slot):
        routes = ring_meta[slot, pl.ds(2 * (1 - which), 1), :]
        gates = ring_meta[slot, pl.ds(2 * (1 - which) + 1, 1), :]
        mine = (routes == z.astype(F32)).astype(F32)
        before = dot(jnp.broadcast_to(mine, (8, TOK)).astype(BF16), earlier())[0:1]
        chosen = jnp.where(mine > 0, before, -1.0)
        picked = jnp.where(iota((CAP, TOK), 0) == chosen, gates, 0.0)
        return jnp.sum(picked, axis=1, keepdims=True)

    def back_copy(which, slot, offset):
        return remote(
            final.at[which, slot],
            back.at[which, slot],
            S_BACK + which * 8 + slot,
            at_ring(-offset),
        )

    def send_back(which, group):
        back_copy(which, 2 * group + 1, group + 1).start()

        @pl.when(group > 0)
        def _():
            back_copy(which, 2 * group, -group).start()

        @pl.when(group == 0)
        def _():
            back[which, 0] = final[which, 0]

    def summed(which, group, s):
        rows = pl.ds(s * CAP, CAP)
        left, right = halves(part_in[which, 2 * group + s])
        gate = gates_of(which, 2 * group + s)
        left = gate * (left + own_part[which, group, rows, pl.ds(0, HALF)])
        right = gate * (right + own_part[which, group, rows, pl.ds(HALF, HALF)])
        return left, right

    for copy in metas[2:]:
        copy.wait_recv()
    gain_acc[...] = jnp.zeros_like(gain_acc)

    def finish_backward(group):
        part_copy(BWD, group).wait_recv()
        for s in range(2):
            slot = 2 * group + s
            dn_left, dn_right = summed(BWD, group, s)
            x_left, x_right = halves(landed[XB, slot])
            inverse = inverse_rms(x_left, x_right)
            u_left = dn_left * gain_left
            u_right = dn_right * gain_right
            inner = jnp.sum(u_left * x_left, axis=-1, keepdims=True)
            inner = inner + jnp.sum(u_right * x_right, axis=-1, keepdims=True)
            scale = inverse * inverse * inverse * (inner * (1.0 / D))
            dy_left, dy_right = halves(all_dy[0, slot])
            g_left = dy_left + inverse * u_left - x_left * scale
            g_right = dy_right + inverse * u_right - x_right * scale
            final[BWD, slot] = jnp.concatenate([g_left, g_right], axis=0).astype(BF16)
            gain_acc[:, pl.ds(0, HALF)] += jnp.sum(
                dn_left * x_left * inverse, axis=0, keepdims=True
            )
            gain_acc[:, pl.ds(HALF, HALF)] += jnp.sum(
                dn_right * x_right * inverse, axis=0, keepdims=True
            )
        send_back(BWD, group)

    def forward(group, carry):
        dup_copy(XF, group, 0).wait_recv()
        dup_copy(XF, group, 1).wait_recv()
        gather_rows(lambda j: all_x[0, j], lambda j: all_x[1, j], group, normed, True)
        acc[...] = jnp.zeros_like(acc)

        def hidden(h, inner):
            rows = normed[...]
            a = dot(rows, wg[h])
            b = dot(rows, wu[h])
            act = (a / (1.0 + jnp.exp(-a)) * b).astype(BF16)
            acc[...] += dot(act, wd[h])
            return inner

        lax.fori_loop(0, 2, hidden, 0)
        share(FWD, group)
        finish_backward(group)
        return carry

    lax.fori_loop(0, GROUPS, forward, 0)

    gain_sum[0] = jnp.zeros((32, 128), F32)
    for r in range(28):
        gain_sum[0, r : r + 1, :] = gain_acc[:, r * 128 : (r + 1) * 128]
    gain_ring[z] = gain_sum[0]
    gain_copies = [
        remote(gain_sum.at[0], gain_ring.at[z], S_GAIN + slot, at_ring(offset_of(slot)))
        for slot in range(1, SLOTS)
    ]
    for copy in gain_copies:
        copy.start()

    def finish_forward(group, carry):
        part_copy(FWD, group).wait_recv()
        for s in range(2):
            slot = 2 * group + s
            q_left, q_right = summed(FWD, group, s)
            x_left, x_right = halves(all_x[0, slot])
            chunk = jnp.concatenate([x_left + q_left, x_right + q_right], axis=0)
            final[FWD, slot] = chunk.astype(BF16)
        send_back(FWD, group)
        return carry

    lax.fori_loop(0, GROUPS, finish_forward, 0)

    for copy in gain_copies:
        copy.wait_recv()
    total = gain_ring[0]
    for index in range(1, 8):
        total = total + gain_ring[index]
    gain_sum[1] = total
    twin_copy = remote(gain_sum.at[1], gain_near.at[0], S_GAIN + 8, twin)
    twin_copy.start()

    stores = []

    def collect(which, hbm, routes):
        for slot in range(1, SLOTS):
            back_copy(which, slot, offset_of(slot)).wait_recv()
        base = jnp.broadcast_to(places(routes, z), (TOK, TOK)).T[:, 0:1]
        column = iota((TOK, SLOTS * ROWS), 1)
        picks = jnp.concatenate([column == base, column == base + CAP], axis=0)
        picks = picks.astype(F32).astype(BF16)
        rows = dot(picks, back[which].reshape(SLOTS * ROWS, HALF))
        outs[which] = rows.astype(BF16)
        for half in range(2):
            store = pltpu.make_async_copy(
                outs.at[which, pl.ds(half * TOK, TOK)],
                hbm.at[0, :, pl.ds(half * HALF, HALF)],
                local_sem.at[9 + which * 2 + half],
            )
            store.start()
            stores.append(store)

    collect(BWD, ob_hbm, meta[2:3, :])
    twin_copy.wait_recv()
    gain_sum[2] = gain_sum[1] + gain_near[0]
    pair_sum = remote(gain_sum.at[2], gain_near.at[1], S_GAIN + 9, pair)
    pair_sum.start()
    collect(FWD, of_hbm, meta[0:1, :])
    pair_sum.wait_recv()
    og_ref[...] = gain_sum[2] + gain_near[1]

    for copy in metas + weights + gain_copies + [twin_copy, pair_sum]:
        copy.wait_send()

    def sent_all(group, carry):
        for array in (XB, DY, XF):
            ring_copy(array, 2 * group + 1, group + 1).wait_send()
        for which in (BWD, FWD):
            back_copy(which, 2 * group + 1, group + 1).wait_send()
            part_copy(which, group).wait_send()

        @pl.when(group > 0)
        def _():
            for array in (XB, DY, XF):
                ring_copy(array, 2 * group, -group).wait_send()
            for which in (BWD, FWD):
                back_copy(which, 2 * group, -group).wait_send()

        pair_copy(group).wait_send()
        for array in (DY, XF):
            for other in range(2):
                dup_copy(array, group, other).wait_send()
        return carry

    lax.fori_loop(0, GROUPS, sent_all, 0)
    for store in stores:
        store.wait()


def chunks(*lead):
    return pltpu.VMEM((*lead, SLOTS, ROWS, HALF), BF16)


def body(
    fwd_prev,
    bwd_next,
    bwd_input,
    norm_gain,
    w_gate,
    w_up,
    w_down,
    fwd_routes,
    fwd_gates,
    bwd_routes,
    bwd_gates,
):
    lines = [
        fwd_routes.astype(F32).reshape(1, TOK),
        fwd_gates.reshape(1, TOK),
        bwd_routes.astype(F32).reshape(1, TOK),
        bwd_gates.reshape(1, TOK),
        jnp.zeros((4, TOK), F32),
    ]
    meta = jnp.concatenate(lines, axis=0)
    vmem = pl.BlockSpec(memory_space=pltpu.VMEM)
    anywhere = pl.BlockSpec(memory_space=pl.ANY)
    fwd_out, bwd_grad, gain_grad = pl.pallas_call(
        kernel,
        out_shape=(
            jax.ShapeDtypeStruct(fwd_prev.shape, BF16),
            jax.ShapeDtypeStruct(fwd_prev.shape, BF16),
            jax.ShapeDtypeStruct((32, 128), F32),
        ),
        in_specs=[vmem] * 2 + [anywhere] * 6,
        out_specs=(anywhere, anywhere, vmem),
        scratch_shapes=[
            pltpu.VMEM((3, 2 * TOK, HALF), BF16),
            chunks(3),
            chunks(3),
            chunks(),
            chunks(2),
            chunks(2),
            chunks(2),
            chunks(2),
            pltpu.VMEM((2, GROUPS, ROWS, D), F32),
            chunks(2),
            chunks(2),
            pltpu.VMEM((2, 2 * TOK, HALF), BF16),
            pltpu.VMEM((2, D, SLICE), BF16),
            pltpu.VMEM((2, D, SLICE), BF16),
            pltpu.VMEM((2, SLICE, D), BF16),
            pltpu.VMEM((2 * ROWS, D), BF16),
            pltpu.VMEM((2 * ROWS, D), BF16),
            pltpu.VMEM((2 * ROWS, D), F32),
            pltpu.VMEM((SLOTS, 8, TOK), F32),
            pltpu.VMEM((2, 8, TOK), F32),
            pltpu.VMEM((1, D), F32),
            pltpu.VMEM((8, 32, 128), F32),
            pltpu.VMEM((3, 32, 128), F32),
            pltpu.VMEM((2, 32, 128), F32),
            pltpu.SemaphoreType.DMA((N_SEM,)),
            pltpu.SemaphoreType.DMA((N_SEM,)),
            pltpu.SemaphoreType.DMA((13,)),
        ],
        compiler_params=pltpu.CompilerParams(
            collective_id=0, has_side_effects=True, vmem_limit_bytes=62 * 2**20
        ),
    )(meta, norm_gain, fwd_prev, bwd_next, bwd_input, w_gate, w_up, w_down)
    return (fwd_out, bwd_grad, gain_grad[:28].reshape(1, D))


def solution(mesh):
    rows = P("pipe", "expert", None)
    columns = P("pipe", None, "expert")
    placed = (rows, rows, rows, P("pipe", None), columns, columns, rows, rows, rows, rows, rows)
    return jax.shard_map(
        body,
        mesh=mesh,
        in_specs=placed,
        out_specs=(rows, rows, P("pipe", None)),
        check_vma=False,
    )
```

time: 807 us -> 255 us (0.32)
  the two profiles are of different devices: /device:TPU:10 before, /device:TPU:34 now
where the time goes in v1:
time: 255 us
  Pallas kernels  248 us (97%)
  local copies, waits for them, and re-layouts  5.78 us (2%)
    pallas_call x1, Pallas kernels, body(): pl.pallas_call(kernel, out_shape=(jax.ShapeDtypeStruct(fwd_prev.shape, BF...  248 us

profile of v1, /device:TPU:34, one launch (start us, length us, event | category | flops | bytes accessed | tf_op | source)
XLA Modules:
  0.0 254.9 jit_solution(3103169836049309412)
XLA Ops:
  0.6 0.7 convert_bitcast_fusion
  1.3 1.3 concatenate.3.meta
  2.6 247.8 %shard_map.130 = (bf16[1,128,3584]{2,1,0:T(8,128)(2,1)}, bf16[1,128,3584]{2,1,0:T(8,128)(2,1)}, f32[32,128]{1,0:T(8,128)}) custom-call(f32[8,128]{1,0:T(8,128)} %concatenate.3.meta, f32[1,3584]{1,0:T(1,128)} %gain.1, bf16[1,128,3584]{2,1,0:T(8,128)(2,1)} %x_hbm.1, bf16[1,128,3584]{2,1,0:T(8,128)(2,1)} %dy_hbm.1, bf16[1,128,3584]{2,1,0:T(8,128)(2,1)} %xb_hbm.1, ...), custom_call_target="tpu_custom_call" | custom-call | tf_op jit(solution)/shard_map/pallas_call | solution.py:528
  250.4 0.0 copy-start
  250.4 0.8 slice_bitcast_fusion
  251.2 0.6 copy.16
  251.8 2.2 copy.19
  253.9 0.0 copy-done
  253.9 0.9 copy.20
  (1 shorter events, 0.0 us)
Async XLA Ops:
  250.4 3.6 %copy-start = (bf16[1,128,3584]{2,1,0:T(8,128)(2,1)S(1)}, bf16[1,128,3584]{2,1,0:T(8,128)(2,1)}, u32[]{:S(2)}) copy-start(bf16[1,128,3584]{2,1,0:T(8,128)(2,1)} %get-tuple-element.15) | copy-start | bytes 2752516

commit v2 on v1

--- a/solution.py
+++ b/solution.py
@@ -16,6 +16,7 @@
 CAP = 24
 ROWS = 2 * CAP
 SLICE = 256
+STAY = 2
 SLOTS = 8
 GROUPS = SLOTS // 2
 PIPE = 8
@@ -31,7 +32,8 @@
 S_PART = 56
 S_BACK = 64
 S_GAIN = 80
-N_SEM = 90
+S_META_RING = 90
+N_SEM = 98
 
 
 def dot(left, right):
@@ -67,13 +69,22 @@
     position = jnp.sum(onehot * before, axis=0, keepdims=True)
     ahead = routes - z.astype(F32)
     ahead = jnp.where(ahead < 0, ahead + 8, ahead)
-    slot = jnp.where(ahead <= 4, 2 * ahead - 1, 2 * (8 - ahead))
-    slot = jnp.where(ahead == 0, 0.0, slot)
+    near = jnp.minimum(ahead, 8 - ahead)
+    group = jnp.where(near == 2, 0.0, jnp.where(near == 3, 2.0, jnp.where(near == 1, 3.0, 1.0)))
+    slot = 2 * group + jnp.where(ahead >= 4, 1.0, 0.0)
     return slot * ROWS + position
 
 
+def offsets(group):
+    first = (2 + 3 * group) % 5
+    return first, 4 * ((4 - first) // 4) - first
+
+
 def kernel(
-    meta,
+    routes_f,
+    gates_f,
+    routes_b,
+    gates_b,
     gain,
     x_hbm,
     dy_hbm,
@@ -102,12 +113,14 @@
     normed,
     grads,
     acc,
+    meta,
     ring_meta,
     near_meta,
     gain_acc,
     gain_ring,
     gain_sum,
     gain_near,
+    picked,
     send_sem,
     recv_sem,
     local_sem,
@@ -117,16 +130,24 @@
     z = place // 4
     xh = (place // 2) % 2
     core = place % 2
-
-    def at_ring(offset):
-        return {"pipe": pipe, "expert": lax.rem(z + offset + 8, 8) * 4 + xh * 2 + core}
+    odd = pipe % 2
+    even = 1 - odd
+
+    def at_ring(offset, ahead=0):
+        return {
+            "pipe": lax.rem(pipe + ahead + PIPE, PIPE),
+            "expert": lax.rem(z + offset + 8, 8) * 4 + xh * 2 + core,
+        }
 
     pair = {"pipe": pipe, "expert": z * 4 + (1 - xh) * 2 + core}
     twin = {"pipe": pipe, "expert": z * 4 + xh * 2 + (1 - core)}
 
-    def at_section(distance, other):
+    def at_section(distance):
+        return {"pipe": lax.rem(pipe + distance + PIPE, PIPE), "expert": place}
+
+    def beside(other):
         side = (1 - xh) if other else xh
-        return {"pipe": lax.rem(pipe + distance + PIPE, PIPE), "expert": z * 4 + side * 2 + core}
+        return {"pipe": pipe + 1 - 2 * odd, "expert": z * 4 + side * 2 + core}
 
     def remote(src, dst, sem, device):
         return pltpu.make_async_remote_copy(
@@ -155,41 +176,58 @@
 
     barrier = pltpu.get_barrier_semaphore()
     partners = [at_ring(k) for k in range(1, 8)] + [pair, twin]
-    for distance in (-1, 1):
-        partners += [at_section(distance, False), at_section(distance, True)]
+    partners += [beside(0), beside(1), at_section(2 * odd - 1)]
+    partners += [at_ring(k, ahead) for ahead in (-2, 2) for k in range(8)]
     for device in partners:
         pl.semaphore_signal(barrier, inc=1, device_id=device, device_id_type=MESH)
-    pl.semaphore_wait(barrier, len(partners))
+
+    meta[...] = jnp.zeros_like(meta)
+    for line, ref in enumerate((routes_f, gates_f, routes_b, gates_b)):
+        meta[line : line + 1, :] = ref[...].astype(F32)
 
     def offset_of(slot):
-        return (slot + 1) // 2 if slot % 2 else -(slot // 2)
+        return offsets(slot // 2)[slot % 2]
+
+    others = [slot for slot in range(SLOTS) if offset_of(slot)]
 
     metas = [
-        remote(meta, near_meta.at[0], S_META, at_section(-1, False)),
-        remote(meta, near_meta.at[1], S_META + 1, at_section(1, False)),
+        remote(meta, near_meta.at[0], S_META, at_section(-1)),
+        remote(meta, near_meta.at[1], S_META + 1, at_section(1)),
     ]
-    for slot in range(1, SLOTS):
+    for slot in others:
         metas.append(
-            remote(meta, ring_meta.at[slot], S_META + 1 + slot, at_ring(offset_of(slot)))
+            remote(meta, ring_meta.at[slot], S_META_RING + slot, at_ring(offset_of(slot)))
         )
-    for copy in metas:
-        copy.start()
-    ring_meta[0] = meta[...]
-
     weights = [
         remote(hbm.at[0], vmem.at[1], S_WEIGHT + index, twin)
         for index, (hbm, vmem) in enumerate(((wg_hbm, wg), (wu_hbm, wu), (wd_hbm, wd)))
     ]
+
+    ahead_of = (0, -2 * even, 2 * odd)
 
     def ring_copy(array, slot, offset):
         return remote(
             sent.at[array, slot],
             landed.at[array, slot],
             S_RING + array * 8 + slot,
-            at_ring(offset),
+            at_ring(offset, ahead_of[array]),
         )
 
-    def dispatch(array, routes):
+    def each_ring(array, group, act, stay=lambda: None):
+        one, two = offsets(group)
+        act(ring_copy(array, 2 * group + 1, two))
+        moved = (0, even, odd)[array]
+        goes = (one != 0) if array == XB else (one != 0) | (moved == 1)
+
+        @pl.when(goes)
+        def _():
+            act(ring_copy(array, 2 * group, one))
+
+        @pl.when(jnp.logical_not(goes))
+        def _():
+            stay()
+
+    def prepare(array, routes):
         base = places(routes, z)
 
         def step(group, carry):
@@ -198,37 +236,32 @@
             picks = picks.astype(F32).astype(BF16)
             rows = dot(picks, raw[array]).astype(BF16)
             sent[array, pl.ds(2 * group, 2)] = rows.reshape(2, ROWS, HALF)
-            ring_copy(array, 2 * group + 1, group + 1).start()
-
-            @pl.when(group > 0)
-            def _():
-                ring_copy(array, 2 * group, -group).start()
-
             return carry
 
         lax.fori_loop(0, GROUPS, step, 0)
-        landed[array, 0] = sent[array, 0]
+
+    def send_group(array, group):
+        def keep():
+            landed[array, STAY] = sent[array, STAY]
+
+        each_ring(array, group, lambda copy: copy.start(), keep)
 
     def wait_landed(array, group):
-        ring_copy(array, 2 * group + 1, group + 1).wait_recv()
-
-        @pl.when(group > 0)
-        def _():
-            ring_copy(array, 2 * group, -group).wait_recv()
+        each_ring(array, group, lambda copy: copy.wait_recv())
 
     loads[0].wait()
     loads[1].wait()
-    dispatch(XB, meta[2:3, :])
-    for copy in weights:
+    prepare(XB, meta[2:3, :])
+    pl.semaphore_wait(barrier, len(partners))
+    for group in (3, 0, 1, 2):
+        send_group(XB, group)
+    for copy in metas + weights:
         copy.start()
+    ring_meta[STAY] = meta[...]
     metas[1].wait_recv()
     loads[2].wait()
     loads[3].wait()
-    dispatch(DY, near_meta[1, 2:3, :])
-    metas[0].wait_recv()
-    loads[4].wait()
-    loads[5].wait()
-    dispatch(XF, near_meta[0, 0:1, :])
+    prepare(DY, near_meta[1, 2:3, :])
 
     def pair_copy(group):
         two = pl.ds(2 * group, 2)
@@ -238,25 +271,46 @@
         two = pl.ds(2 * group, 2)
         dst = all_dy if array == DY else all_x
         sem = S_DUP + (array - 1) * 8 + other * 4 + group
-        device = at_section(-1 if array == DY else 1, other)
-        return remote(landed.at[array, two], dst.at[other, two], sem, device)
-
-    def relay_pair(group, carry):
+        return remote(landed.at[array, two], dst.at[other, two], sem, beside(other))
+
+    def relay_pair(group):
         wait_landed(XB, group)
         pair_copy(group).start()
-        return carry
 
     def relay_dup(array, group):
         wait_landed(array, group)
         dup_copy(array, group, 0).start()
         dup_copy(array, group, 1).start()
 
-    def relay_dy(group, carry):
-        relay_dup(DY, group)
-        return carry
-
-    lax.fori_loop(0, GROUPS, relay_pair, 0)
-    lax.fori_loop(0, GROUPS, relay_dy, 0)
+    def prepare_collect(which, routes):
+        base = jnp.broadcast_to(places(routes, z), (TOK, TOK)).T[:, 0:1]
+        column = iota((TOK, SLOTS * ROWS), 1)
+        picks = jnp.concatenate([column == base, column == base + CAP], axis=0)
+        picked[which] = picks.astype(F32).astype(BF16)
+
+    relay_pair(3)
+    relay_pair(0)
+    send_group(DY, 0)
+    send_group(DY, 1)
+    send_group(DY, 2)
+    send_group(DY, 3)
+    metas[0].wait_recv()
+    loads[4].wait()
+    loads[5].wait()
+    prepare(XF, near_meta[0, 0:1, :])
+    relay_pair(1)
+    relay_pair(2)
+    relay_dup(DY, 0)
+    relay_dup(DY, 1)
+    send_group(XF, 0)
+    send_group(XF, 1)
+    send_group(XF, 2)
+    send_group(XF, 3)
+    relay_dup(DY, 2)
+    relay_dup(DY, 3)
+
+    prepare_collect(FWD, meta[0:1, :])
+    prepare_collect(BWD, meta[2:3, :])
 
     gain_left = gain[:, :HALF]
     gain_right = gain[:, HALF:]
@@ -295,34 +349,6 @@
     for copy in weights:
         copy.wait_recv()
 
-    def backward(group, carry):
-        relay_dup(XF, group)
-        pair_copy(group).wait_recv()
-        dup_copy(DY, group, 0).wait_recv()
-        dup_copy(DY, group, 1).wait_recv()
-        gather_rows(
-            lambda j: landed[XB, j], lambda j: pair_xb[j], group, normed, True
-        )
-        gather_rows(lambda j: all_dy[0, j], lambda j: all_dy[1, j], group, grads, False)
-        acc[...] = jnp.zeros_like(acc)
-
-        def hidden(h, inner):
-            rows = normed[...]
-            a = dot(rows, wg[h])
-            b = dot(rows, wu[h])
-            dh = contract_last(grads[...], wd[h])
-            sig = 1.0 / (1.0 + jnp.exp(-a))
-            da = (dh * b * sig * (1.0 + a * (1.0 - sig))).astype(BF16)
-            db = (dh * a * sig).astype(BF16)
-            acc[...] += contract_last(da, wg[h]) + contract_last(db, wu[h])
-            return inner
-
-        lax.fori_loop(0, 2, hidden, 0)
-        share(BWD, group)
-        return carry
-
-    lax.fori_loop(0, GROUPS, backward, 0)
-
     def gates_of(which, slot):
         routes = ring_meta[slot, pl.ds(2 * (1 - which), 1), :]
         gates = ring_meta[slot, pl.ds(2 * (1 - which) + 1, 1), :]
@@ -340,16 +366,23 @@
             at_ring(-offset),
         )
 
+    def each_back(which, group, act, stay=lambda: None):
+        one, two = offsets(group)
+        act(back_copy(which, 2 * group + 1, two))
+
+        @pl.when(one != 0)
+        def _():
+            act(back_copy(which, 2 * group, one))
+
+        @pl.when(one == 0)
+        def _():
+            stay()
+
     def send_back(which, group):
-        back_copy(which, 2 * group + 1, group + 1).start()
-
-        @pl.when(group > 0)
-        def _():
-            back_copy(which, 2 * group, -group).start()
-
-        @pl.when(group == 0)
-        def _():
-            back[which, 0] = final[which, 0]
+        def keep():
+            back[which, STAY] = final[which, STAY]
+
+        each_back(which, group, lambda copy: copy.start(), keep)
 
     def summed(which, group, s):
         rows = pl.ds(s * CAP, CAP)
@@ -359,8 +392,16 @@
         right = gate * (right + own_part[which, group, rows, pl.ds(HALF, HALF)])
         return left, right
 
-    for copy in metas[2:]:
-        copy.wait_recv()
+    def finish_forward(group):
+        part_copy(FWD, group).wait_recv()
+        for s in range(2):
+            slot = 2 * group + s
+            q_left, q_right = summed(FWD, group, s)
+            x_left, x_right = halves(all_x[0, slot])
+            chunk = jnp.concatenate([x_left + q_left, x_right + q_right], axis=0)
+            final[FWD, slot] = chunk.astype(BF16)
+        send_back(FWD, group)
+
     gain_acc[...] = jnp.zeros_like(gain_acc)
 
     def finish_backward(group):
@@ -387,6 +428,38 @@
             )
         send_back(BWD, group)
 
+    def backward(group, carry):
+        pair_copy(group).wait_recv()
+        dup_copy(DY, group, 0).wait_recv()
+        dup_copy(DY, group, 1).wait_recv()
+        gather_rows(
+            lambda j: landed[XB, j], lambda j: pair_xb[j], group, normed, True
+        )
+        gather_rows(lambda j: all_dy[0, j], lambda j: all_dy[1, j], group, grads, False)
+        acc[...] = jnp.zeros_like(acc)
+
+        def hidden(h, inner):
+            rows = normed[...]
+            a = dot(rows, wg[h])
+            b = dot(rows, wu[h])
+            dh = contract_last(grads[...], wd[h])
+            sig = 1.0 / (1.0 + jnp.exp(-a))
+            da = (dh * b * sig * (1.0 + a * (1.0 - sig))).astype(BF16)
+            db = (dh * a * sig).astype(BF16)
+            acc[...] += contract_last(da, wg[h]) + contract_last(db, wu[h])
+            return inner
+
+        lax.fori_loop(0, 2, hidden, 0)
+        share(BWD, group)
+        relay_dup(XF, group)
+
+        return carry
+
+    lax.fori_loop(0, GROUPS, backward, 0)
+
+    for copy in metas[2:]:
+        copy.wait_recv()
+
     def forward(group, carry):
         dup_copy(XF, group, 0).wait_recv()
         dup_copy(XF, group, 1).wait_recv()
@@ -408,30 +481,34 @@
 
     lax.fori_loop(0, GROUPS, forward, 0)
 
+
     gain_sum[0] = jnp.zeros((32, 128), F32)
     for r in range(28):
         gain_sum[0, r : r + 1, :] = gain_acc[:, r * 128 : (r + 1) * 128]
     gain_ring[z] = gain_sum[0]
     gain_copies = [
         remote(gain_sum.at[0], gain_ring.at[z], S_GAIN + slot, at_ring(offset_of(slot)))
-        for slot in range(1, SLOTS)
+        for slot in others
     ]
     for copy in gain_copies:
         copy.start()
 
-    def finish_forward(group, carry):
-        part_copy(FWD, group).wait_recv()
-        for s in range(2):
-            slot = 2 * group + s
-            q_left, q_right = summed(FWD, group, s)
-            x_left, x_right = halves(all_x[0, slot])
-            chunk = jnp.concatenate([x_left + q_left, x_right + q_right], axis=0)
-            final[FWD, slot] = chunk.astype(BF16)
-        send_back(FWD, group)
+    for copy in metas + weights:
+        copy.wait_send()
+
+    def first_sent(group, carry):
+        for array in (XB, DY, XF):
+            each_ring(array, group, lambda copy: copy.wait_send())
+        pair_copy(group).wait_send()
+        for array in (DY, XF):
+            for other in range(2):
+                dup_copy(array, group, other).wait_send()
         return carry
 
-    lax.fori_loop(0, GROUPS, finish_forward, 0)
-
+    lax.fori_loop(0, GROUPS, first_sent, 0)
+
+    finish_forward(0)
+    finish_forward(1)
     for copy in gain_copies:
         copy.wait_recv()
     total = gain_ring[0]
@@ -440,17 +517,19 @@
     gain_sum[1] = total
     twin_copy = remote(gain_sum.at[1], gain_near.at[0], S_GAIN + 8, twin)
     twin_copy.start()
+    finish_forward(2)
+    twin_copy.wait_recv()
+    gain_sum[2] = gain_sum[1] + gain_near[0]
+    pair_sum = remote(gain_sum.at[2], gain_near.at[1], S_GAIN + 9, pair)
+    pair_sum.start()
+    finish_forward(3)
 
     stores = []
 
-    def collect(which, hbm, routes):
-        for slot in range(1, SLOTS):
+    def collect(which, hbm):
+        for slot in others:
             back_copy(which, slot, offset_of(slot)).wait_recv()
-        base = jnp.broadcast_to(places(routes, z), (TOK, TOK)).T[:, 0:1]
-        column = iota((TOK, SLOTS * ROWS), 1)
-        picks = jnp.concatenate([column == base, column == base + CAP], axis=0)
-        picks = picks.astype(F32).astype(BF16)
-        rows = dot(picks, back[which].reshape(SLOTS * ROWS, HALF))
+        rows = dot(picked[which], back[which].reshape(SLOTS * ROWS, HALF))
         outs[which] = rows.astype(BF16)
         for half in range(2):
             store = pltpu.make_async_copy(
@@ -461,39 +540,23 @@
             store.start()
             stores.append(store)
 
-    collect(BWD, ob_hbm, meta[2:3, :])
-    twin_copy.wait_recv()
-    gain_sum[2] = gain_sum[1] + gain_near[0]
-    pair_sum = remote(gain_sum.at[2], gain_near.at[1], S_GAIN + 9, pair)
-    pair_sum.start()
-    collect(FWD, of_hbm, meta[0:1, :])
+    collect(BWD, ob_hbm)
+    collect(FWD, of_hbm)
     pair_sum.wait_recv()
-    og_ref[...] = gain_sum[2] + gain_near[1]
-
-    for copy in metas + weights + gain_copies + [twin_copy, pair_sum]:
+    total = gain_sum[2] + gain_near[1]
+    for r in range(28):
+        og_ref[:, r * 128 : (r + 1) * 128] = total[r : r + 1, :]
+
+    for copy in gain_copies + [twin_copy, pair_sum]:
         copy.wait_send()
 
-    def sent_all(group, carry):
-        for array in (XB, DY, XF):
-            ring_copy(array, 2 * group + 1, group + 1).wait_send()
+    def last_sent(group, carry):
         for which in (BWD, FWD):
-            back_copy(which, 2 * group + 1, group + 1).wait_send()
+            each_back(which, group, lambda copy: copy.wait_send())
             part_copy(which, group).wait_send()
-
-        @pl.when(group > 0)
-        def _():
-            for array in (XB, DY, XF):
-                ring_copy(array, 2 * group, -group).wait_send()
-            for which in (BWD, FWD):
-                back_copy(which, 2 * group, -group).wait_send()
-
-        pair_copy(group).wait_send()
-        for array in (DY, XF):
-            for other in range(2):
-                dup_copy(array, group, other).wait_send()
         return carry
 
-    lax.fori_loop(0, GROUPS, sent_all, 0)
+    lax.fori_loop(0, GROUPS, last_sent, 0)
     for store in stores:
         store.wait()
 
@@ -515,14 +578,7 @@
     bwd_routes,
     bwd_gates,
 ):
-    lines = [
-        fwd_routes.astype(F32).reshape(1, TOK),
-        fwd_gates.reshape(1, TOK),
-        bwd_routes.astype(F32).reshape(1, TOK),
-        bwd_gates.reshape(1, TOK),
-        jnp.zeros((4, TOK), F32),
-    ]
-    meta = jnp.concatenate(lines, axis=0)
+    lines = [v.reshape(1, TOK) for v in (fwd_routes, fwd_gates, bwd_routes, bwd_gates)]
     vmem = pl.BlockSpec(memory_space=pltpu.VMEM)
     anywhere = pl.BlockSpec(memory_space=pl.ANY)
     fwd_out, bwd_grad, gain_grad = pl.pallas_call(
@@ -530,9 +586,9 @@
         out_shape=(
             jax.ShapeDtypeStruct(fwd_prev.shape, BF16),
             jax.ShapeDtypeStruct(fwd_prev.shape, BF16),
-            jax.ShapeDtypeStruct((32, 128), F32),
+            jax.ShapeDtypeStruct((1, D), F32),
         ),
-        in_specs=[vmem] * 2 + [anywhere] * 6,
+        in_specs=[vmem] * 5 + [anywhere] * 6,
         out_specs=(anywhere, anywhere, vmem),
         scratch_shapes=[
             pltpu.VMEM((3, 2 * TOK, HALF), BF16),
@@ -553,12 +609,14 @@
             pltpu.VMEM((2 * ROWS, D), BF16),
             pltpu.VMEM((2 * ROWS, D), BF16),
             pltpu.VMEM((2 * ROWS, D), F32),
+            pltpu.VMEM((8, TOK), F32),
             pltpu.VMEM((SLOTS, 8, TOK), F32),
             pltpu.VMEM((2, 8, TOK), F32),
             pltpu.VMEM((1, D), F32),
             pltpu.VMEM((8, 32, 128), F32),
             pltpu.VMEM((3, 32, 128), F32),
             pltpu.VMEM((2, 32, 128), F32),
+            pltpu.VMEM((2, 2 * TOK, SLOTS * ROWS), BF16),
             pltpu.SemaphoreType.DMA((N_SEM,)),
             pltpu.SemaphoreType.DMA((N_SEM,)),
             pltpu.SemaphoreType.DMA((13,)),
@@ -566,8 +624,8 @@
         compiler_params=pltpu.CompilerParams(
             collective_id=0, has_side_effects=True, vmem_limit_bytes=62 * 2**20
         ),
-    )(meta, norm_gain, fwd_prev, bwd_next, bwd_input, w_gate, w_up, w_down)
-    return (fwd_out, bwd_grad, gain_grad[:28].reshape(1, D))
+    )(*lines, norm_gain, fwd_prev, bwd_next, bwd_input, w_gate, w_up, w_down)
+    return (fwd_out, bwd_grad, gain_grad)
 
 
 def solution(mesh):

time: 255 us -> 210 us (0.82)
  the two profiles are of different devices: /device:TPU:34 before, /device:TPU:10 now
where the time goes in v2:
time: 210 us
  Pallas kernels  205 us (98%)
  local copies, waits for them, and re-layouts  3.77 us (2%)
    pallas_call x1, Pallas kernels, body(): pl.pallas_call(kernel, out_shape=(jax.ShapeDtypeStruct(fwd_prev.shape, BF...  205 us

profile of v2, /device:TPU:10, one launch (start us, length us, event | category | flops | bytes accessed | tf_op | source)
XLA Modules:
  0.0 209.6 jit_solution(9879417067413255925)
XLA Ops:
  0.6 205.1 %shard_map.130 = (bf16[1,128,3584]{2,1,0:T(8,128)(2,1)}, bf16[1,128,3584]{2,1,0:T(8,128)(2,1)}, f32[1,3584]{1,0:T(1,128)}) custom-call(s32[1,128]{1,0:T(1,128)} %bitcast.4, f32[1,128]{1,0:T(1,128)} %bitcast.5, s32[1,128]{1,0:T(1,128)} %bitcast.6, f32[1,128]{1,0:T(1,128)} %bitcast.7, f32[1,3584]{1,0:T(1,128)} %gain.1, bf16[1,128,3584]{2,1,0:T(8,128)(2,1)} %x_hbm.1, ...), custom_call_target="tpu_custom_call" | custom-call | tf_op jit(solution)/shard_map/pallas_call | solution.py:584
  205.8 0.0 copy-start
  205.8 0.0 copy-start.1
  205.8 2.2 %copy.17 = bf16[1,128,3584]{2,1,0:T(8,128)(2,1)} copy(bf16[1,128,3584]{2,1,0:T(8,128)(2,1)} %get-tuple-element.6) | data formatting | bytes 1835008
  208.0 0.0 copy-done
  208.0 0.9 copy.18
  209.0 0.0 copy-done.1
  209.0 0.6 copy.19
Async XLA Ops:
  205.8 2.3 %copy-start = (bf16[1,128,3584]{2,1,0:T(8,128)(2,1)S(1)}, bf16[1,128,3584]{2,1,0:T(8,128)(2,1)}, u32[]{:S(2)}) copy-start(bf16[1,128,3584]{2,1,0:T(8,128)(2,1)} %get-tuple-element.7) | copy-start | bytes 2752516
  205.8 3.2 %copy-start.1 = (f32[1,3584]{1,0:T(1,128)S(1)}, f32[1,3584]{1,0:T(1,128)}, u32[]{:S(2)}) copy-start(f32[1,3584]{1,0:T(1,128)} %get-tuple-element.8) | copy-start | bytes 43012

commit v3 on v2

--- a/solution.py
+++ b/solution.py
@@ -16,6 +16,7 @@
 CAP = 24
 ROWS = 2 * CAP
 SLICE = 256
+AHEAD = 2
 STAY = 2
 SLOTS = 8
 GROUPS = SLOTS // 2
@@ -29,11 +30,11 @@
 S_RING = 12
 S_PAIR = 36
 S_DUP = 40
-S_PART = 56
+S_PART = 98
 S_BACK = 64
 S_GAIN = 80
 S_META_RING = 90
-N_SEM = 98
+N_SEM = 114
 
 
 def dot(left, right):
@@ -120,7 +121,9 @@
     gain_ring,
     gain_sum,
     gain_near,
-    picked,
+    gate_cols,
+    picked_first,
+    picked_last,
     send_sem,
     recv_sem,
     local_sem,
@@ -284,9 +287,10 @@
 
     def prepare_collect(which, routes):
         base = jnp.broadcast_to(places(routes, z), (TOK, TOK)).T[:, 0:1]
-        column = iota((TOK, SLOTS * ROWS), 1)
-        picks = jnp.concatenate([column == base, column == base + CAP], axis=0)
-        picked[which] = picks.astype(F32).astype(BF16)
+        for first, ref in ((0, picked_first), (6, picked_last)):
+            column = iota((TOK, ref.shape[-1]), 1) + first * ROWS
+            picks = jnp.concatenate([column == base, column == base + CAP], axis=0)
+            ref[which] = picks.astype(F32).astype(BF16)
 
     relay_pair(3)
     relay_pair(0)
@@ -309,6 +313,23 @@
     relay_dup(DY, 2)
     relay_dup(DY, 3)
 
+    def prepare_gates(which):
+        line = 2 * (1 - which)
+        routes = ring_meta[:, line, :]
+        gates = ring_meta[:, line + 1, :]
+        mine = (routes == z.astype(F32)).astype(F32)
+        before = dot(mine.astype(BF16), earlier())
+        chosen = jnp.where(mine > 0, before, -1.0)
+        for slot in range(SLOTS):
+            one = slice(slot, slot + 1)
+            found = jnp.where(iota((CAP, TOK), 0) == chosen[one], gates[one], 0.0)
+            column = jnp.sum(found, axis=1, keepdims=True)
+            gate_cols[which, slot] = jnp.broadcast_to(column, (CAP, TOK))
+
+    for copy in metas[2:]:
+        copy.wait_recv()
+    prepare_gates(BWD)
+    prepare_gates(FWD)
     prepare_collect(FWD, meta[0:1, :])
     prepare_collect(BWD, meta[2:3, :])
 
@@ -330,33 +351,31 @@
             to[rows, pl.ds(0, HALF)] = jnp.concatenate(lefts, axis=0).astype(BF16)
             to[rows, pl.ds(HALF, HALF)] = jnp.concatenate(rights, axis=0).astype(BF16)
 
-    def part_copy(which, group):
-        two = pl.ds(2 * group, 2)
+    def part_copy(which, slot):
         return remote(
-            part_out.at[which, two], part_in.at[which, two], S_PART + which * 4 + group, pair
+            part_out.at[which, slot], part_in.at[which, slot], S_PART + which * 8 + slot, pair
         )
 
-    def share(which, group):
-        own_part[which, group] = acc[pl.ds(0, ROWS), :]
+    def share(which, group, start):
         for s in range(2):
             rows = pl.ds(ROWS + s * CAP, CAP)
             chunk = jnp.concatenate([acc[rows, pl.ds(0, HALF)], acc[rows, pl.ds(HALF, HALF)]], axis=0)
             part_out[which, 2 * group + s] = chunk.astype(BF16)
-        part_copy(which, group).start()
+            if start is True:
+                part_copy(which, 2 * group + s).start()
+        if start is not True:
+
+            @pl.when(start)
+            def _():
+                part_copy(which, 2 * group).start()
+                part_copy(which, 2 * group + 1).start()
+
+        own_part[which, group] = acc[pl.ds(0, ROWS), :]
 
     for load in loads[6:]:
         load.wait()
     for copy in weights:
         copy.wait_recv()
-
-    def gates_of(which, slot):
-        routes = ring_meta[slot, pl.ds(2 * (1 - which), 1), :]
-        gates = ring_meta[slot, pl.ds(2 * (1 - which) + 1, 1), :]
-        mine = (routes == z.astype(F32)).astype(F32)
-        before = dot(jnp.broadcast_to(mine, (8, TOK)).astype(BF16), earlier())[0:1]
-        chosen = jnp.where(mine > 0, before, -1.0)
-        picked = jnp.where(iota((CAP, TOK), 0) == chosen, gates, 0.0)
-        return jnp.sum(picked, axis=1, keepdims=True)
 
     def back_copy(which, slot, offset):
         return remote(
@@ -366,9 +385,11 @@
             at_ring(-offset),
         )
 
-    def each_back(which, group, act, stay=lambda: None):
+    def each_back(which, group, s, act, stay=lambda: None):
         one, two = offsets(group)
-        act(back_copy(which, 2 * group + 1, two))
+        if s == 1:
+            act(back_copy(which, 2 * group + 1, two))
+            return
 
         @pl.when(one != 0)
         def _():
@@ -378,36 +399,36 @@
         def _():
             stay()
 
-    def send_back(which, group):
+    def send_back(which, group, s):
         def keep():
             back[which, STAY] = final[which, STAY]
 
-        each_back(which, group, lambda copy: copy.start(), keep)
+        each_back(which, group, s, lambda copy: copy.start(), keep)
 
     def summed(which, group, s):
         rows = pl.ds(s * CAP, CAP)
         left, right = halves(part_in[which, 2 * group + s])
-        gate = gates_of(which, 2 * group + s)
+        gate = gate_cols[which, 2 * group + s, :, 0:1]
         left = gate * (left + own_part[which, group, rows, pl.ds(0, HALF)])
         right = gate * (right + own_part[which, group, rows, pl.ds(HALF, HALF)])
         return left, right
 
-    def finish_forward(group):
-        part_copy(FWD, group).wait_recv()
+    def finish_forward(slot):
+        part_copy(FWD, slot).wait_recv()
+        if slot + AHEAD < SLOTS:
+            part_copy(FWD, slot + AHEAD).start()
+        q_left, q_right = summed(FWD, slot // 2, slot % 2)
+        x_left, x_right = halves(all_x[0, slot])
+        chunk = jnp.concatenate([x_left + q_left, x_right + q_right], axis=0)
+        final[FWD, slot] = chunk.astype(BF16)
+        send_back(FWD, slot // 2, slot % 2)
+
+    gain_acc[...] = jnp.zeros_like(gain_acc)
+
+    def finish_backward(group):
         for s in range(2):
             slot = 2 * group + s
-            q_left, q_right = summed(FWD, group, s)
-            x_left, x_right = halves(all_x[0, slot])
-            chunk = jnp.concatenate([x_left + q_left, x_right + q_right], axis=0)
-            final[FWD, slot] = chunk.astype(BF16)
-        send_back(FWD, group)
-
-    gain_acc[...] = jnp.zeros_like(gain_acc)
-
-    def finish_backward(group):
-        part_copy(BWD, group).wait_recv()
-        for s in range(2):
-            slot = 2 * group + s
+            part_copy(BWD, slot).wait_recv()
             dn_left, dn_right = summed(BWD, group, s)
             x_left, x_right = halves(landed[XB, slot])
             inverse = inverse_rms(x_left, x_right)
@@ -420,13 +441,13 @@
             g_left = dy_left + inverse * u_left - x_left * scale
             g_right = dy_right + inverse * u_right - x_right * scale
             final[BWD, slot] = jnp.concatenate([g_left, g_right], axis=0).astype(BF16)
+            send_back(BWD, group, s)
             gain_acc[:, pl.ds(0, HALF)] += jnp.sum(
                 dn_left * x_left * inverse, axis=0, keepdims=True
             )
             gain_acc[:, pl.ds(HALF, HALF)] += jnp.sum(
                 dn_right * x_right * inverse, axis=0, keepdims=True
             )
-        send_back(BWD, group)
 
     def backward(group, carry):
         pair_copy(group).wait_recv()
@@ -450,15 +471,12 @@
             return inner
 
         lax.fori_loop(0, 2, hidden, 0)
-        share(BWD, group)
+        share(BWD, group, True)
         relay_dup(XF, group)
 
         return carry
 
     lax.fori_loop(0, GROUPS, backward, 0)
-
-    for copy in metas[2:]:
-        copy.wait_recv()
 
     def forward(group, carry):
         dup_copy(XF, group, 0).wait_recv()
@@ -475,7 +493,7 @@
             return inner
 
         lax.fori_loop(0, 2, hidden, 0)
-        share(FWD, group)
+        share(FWD, group, group == 0)
         finish_backward(group)
         return carry
 
@@ -507,8 +525,10 @@
 
     lax.fori_loop(0, GROUPS, first_sent, 0)
 
-    finish_forward(0)
-    finish_forward(1)
+    for slot in range(2, AHEAD):
+        part_copy(FWD, slot).start()
+    for slot in range(4):
+        finish_forward(slot)
     for copy in gain_copies:
         copy.wait_recv()
     total = gain_ring[0]
@@ -517,19 +537,24 @@
     gain_sum[1] = total
     twin_copy = remote(gain_sum.at[1], gain_near.at[0], S_GAIN + 8, twin)
     twin_copy.start()
-    finish_forward(2)
+    finish_forward(4)
+    finish_forward(5)
     twin_copy.wait_recv()
     gain_sum[2] = gain_sum[1] + gain_near[0]
     pair_sum = remote(gain_sum.at[2], gain_near.at[1], S_GAIN + 9, pair)
     pair_sum.start()
-    finish_forward(3)
+    finish_forward(6)
+    finish_forward(7)
 
     stores = []
 
     def collect(which, hbm):
-        for slot in others:
+        for slot in others[:-2]:
             back_copy(which, slot, offset_of(slot)).wait_recv()
-        rows = dot(picked[which], back[which].reshape(SLOTS * ROWS, HALF))
+        acc_rows = dot(picked_first[which], back[which, 0:6].reshape(6 * ROWS, HALF))
+        for slot in others[-2:]:
+            back_copy(which, slot, offset_of(slot)).wait_recv()
+        rows = acc_rows + dot(picked_last[which], back[which, 6:8].reshape(2 * ROWS, HALF))
         outs[which] = rows.astype(BF16)
         for half in range(2):
             store = pltpu.make_async_copy(
@@ -552,8 +577,9 @@
 
     def last_sent(group, carry):
         for which in (BWD, FWD):
-            each_back(which, group, lambda copy: copy.wait_send())
-            part_copy(which, group).wait_send()
+            for s in range(2):
+                each_back(which, group, s, lambda copy: copy.wait_send())
+                part_copy(which, 2 * group + s).wait_send()
         return carry
 
     lax.fori_loop(0, GROUPS, last_sent, 0)
@@ -616,7 +642,9 @@
             pltpu.VMEM((8, 32, 128), F32),
             pltpu.VMEM((3, 32, 128), F32),
             pltpu.VMEM((2, 32, 128), F32),
-            pltpu.VMEM((2, 2 * TOK, SLOTS * ROWS), BF16),
+            pltpu.VMEM((2, SLOTS, CAP, TOK), F32),
+            pltpu.VMEM((2, 2 * TOK, 6 * ROWS), BF16),
+            pltpu.VMEM((2, 2 * TOK, 2 * ROWS), BF16),
             pltpu.SemaphoreType.DMA((N_SEM,)),
             pltpu.SemaphoreType.DMA((N_SEM,)),
             pltpu.SemaphoreType.DMA((13,)),

time: 210 us -> 203 us (0.967)
  Pallas kernels: 205 us -> 198 us
    pallas_call x1, Pallas kernels: 205 us -> 198 us  [body(): pl.pallas_call(kernel, out_shape=(jax.ShapeDtypeStruct(fwd_prev.shape, BF...]
where the time goes in v3:
time: 203 us; the launch traced here: 202 us
  Pallas kernels  198 us (98%)
  local copies, waits for them, and re-layouts  3.77 us (2%)
    pallas_call x1, Pallas kernels, body(): pl.pallas_call(kernel, out_shape=(jax.ShapeDtypeStruct(fwd_prev.shape, BF...  198 us

profile of v3, /device:TPU:10, one launch (start us, length us, event | category | flops | bytes accessed | tf_op | source)
XLA Modules:
  0.0 202.4 jit_solution(15798742242704100325)
XLA Ops:
  0.6 198.0 %shard_map.130 = (bf16[1,128,3584]{2,1,0:T(8,128)(2,1)}, bf16[1,128,3584]{2,1,0:T(8,128)(2,1)}, f32[1,3584]{1,0:T(1,128)}) custom-call(s32[1,128]{1,0:T(1,128)} %bitcast.4, f32[1,128]{1,0:T(1,128)} %bitcast.5, s32[1,128]{1,0:T(1,128)} %bitcast.6, f32[1,128]{1,0:T(1,128)} %bitcast.7, f32[1,3584]{1,0:T(1,128)} %gain.1, bf16[1,128,3584]{2,1,0:T(8,128)(2,1)} %x_hbm.1, ...), custom_call_target="tpu_custom_call" | custom-call | tf_op jit(solution)/shard_map/pallas_call | solution.py:610
  198.6 0.0 copy-start
  198.6 0.0 copy-start.1
  198.6 2.2 %copy.17 = bf16[1,128,3584]{2,1,0:T(8,128)(2,1)} copy(bf16[1,128,3584]{2,1,0:T(8,128)(2,1)} %get-tuple-element.6) | data formatting | bytes 1835008
  200.9 0.0 copy-done
  200.9 0.9 copy.18
  201.8 0.0 copy-done.1
  201.8 0.6 copy.19
Async XLA Ops:
  198.6 2.3 %copy-start = (bf16[1,128,3584]{2,1,0:T(8,128)(2,1)S(1)}, bf16[1,128,3584]{2,1,0:T(8,128)(2,1)}, u32[]{:S(2)}) copy-start(bf16[1,128,3584]{2,1,0:T(8,128)(2,1)} %get-tuple-element.7) | copy-start | bytes 2752516
  198.6 3.2 %copy-start.1 = (f32[1,3584]{1,0:T(1,128)S(1)}, f32[1,3584]{1,0:T(1,128)}, u32[]{:S(2)}) copy-start(f32[1,3584]{1,0:T(1,128)} %get-tuple-element.8) | copy-start | bytes 43012
